TPU v7x, 32 devices: a whole 2x2x4 slice. The times are simulated.
32 devices in a mesh: groups: 2 (over x), leaf: 16 (over z, y, core).
Axes of the slice: x: 2, y: 2, z: 4, core: 2. Of those that a mesh axis runs over, the one named last changes fastest.
Arguments:
- right_side: float32 [256, 65536], P('groups', 'leaf'), parts along dimension 0, may hold values from -30 to 30
- point_order: int32 [131072], P(('groups', 'leaf')), parts along dimension 0, may hold values from 0 to 65535, as said below
- leaf_blocks: bfloat16 [128, 512, 512], P('leaf'), may hold values from -0.01 to 6, as said below
- bases: bfloat16 [7, 128, 65536], P(None, None, 'leaf'), may hold values from -4 to 4
- rank_weights: float32 [7, 128], replicated, may hold values from 0.05 to 0.6
Outputs:
- field_solution: float32 [256, 65536], P('groups', 'leaf'), parts along dimension 0
- field_residual: float32 [256, 65536], P('groups', 'leaf'), parts along dimension 0
There are 2 independent parts, one for each index of `groups`. A program takes and returns all parts, laid end to end along the dimension named above; an argument that names none is the same for every part. Nothing has to cross between parts.
Inputs may be any that keep to these rules, and one draw needn't show every extreme that they name: `point_order`: each aligned run of 4096 entries holds each of its own 4096 positions once. `leaf_blocks`: every block is symmetric positive definite.
All inputs are finite; a program needn't handle non-finite values.
Results may differ from a plain program's by a relative error of at most 0.0049.
Values sent between devices are 32-bit elements; how exact they have to be, the bound alone decides.
A program may use at most 128 MiB of HBM per device.

v0:
```python
import math

import jax
import jax.numpy as jnp
from jax import lax
from jax.sharding import PartitionSpec as P

ITERS = 2


def from_partner(array, axis, stride):
    return lax.ppermute(array, axis, [(i, i ^ 1 << stride) for i in range(lax.axis_size(axis))])


def scale_level(values, tree_level, rank_weights, leaf_size):
    rank_size = rank_weights.shape[1]
    factor = 1.0 / math.sqrt(rank_size * leaf_size * 2 ** (tree_level + 1))
    return (values * factor * rank_weights[tree_level]).astype(jnp.bfloat16)


def double_up(stacked):
    finished = []
    pending = stacked
    for tree_bit in range(stacked.shape[0]):
        received = from_partner(pending, "leaf", tree_bit)
        pending = pending + received
        finished.append(pending[0])
        pending = pending[1:]
    return finished


def apply_operator(probe, leaf_blocks, bases, rank_weights):
    columns, points = probe.shape
    blocks, leaf_size = (leaf_blocks.shape[0], leaf_blocks.shape[1])
    levels, rank_size = rank_weights.shape
    upper_levels = lax.axis_size("leaf").bit_length() - 1
    local_levels = levels - upper_levels
    probe_tiles = probe.reshape(columns, blocks, leaf_size)
    basis_tiles = bases.reshape(levels, rank_size, blocks, leaf_size)
    dense_part = jnp.einsum(
        "nbj,bjp->nbp", probe_tiles, leaf_blocks, preferred_element_type=jnp.float32
    )
    partial_value = jnp.einsum(
        "nbp,lrbp->blnr", probe_tiles, basis_tiles, preferred_element_type=jnp.float32
    )
    scaled_levels = []
    for tree_level in range(local_levels):
        per_node = 2 ** (tree_level + 1)
        grouped = (
            partial_value[:, tree_level]
            .reshape(blocks // per_node, per_node, columns, rank_size)
            .sum(axis=1)
        )
        scaled = scale_level(grouped, tree_level, rank_weights, leaf_size)
        scaled_levels.append(jnp.repeat(scaled, per_node, axis=0))
    device_terms = partial_value[:, local_levels:].sum(axis=0)
    level_totals = double_up(device_terms)
    for offset_level, level_total in enumerate(level_totals):
        scaled = scale_level(level_total, local_levels + offset_level, rank_weights, leaf_size)
        scaled_levels.append(jnp.broadcast_to(scaled, (blocks, columns, rank_size)))
    stacked = jnp.stack(scaled_levels)
    low_rank = jnp.einsum(
        "lbnr,lrbp->nbp", stacked, basis_tiles, preferred_element_type=jnp.float32
    )
    return (dense_part + low_rank).reshape(columns, points)


def squares(values):
    return lax.psum(jnp.sum(values * values, axis=1), "leaf")


def on_device(right_side, point_order, leaf_blocks, bases, rank_weights):
    columns, points = right_side.shape
    first_point = lax.axis_index("leaf") * points
    local_order = point_order - first_point
    ordered = jnp.take(right_side, local_order, axis=1)
    solution = jnp.zeros_like(ordered)
    residual = ordered
    direction = ordered
    norm_now = squares(residual)
    for iteration in range(ITERS):
        image_field = apply_operator(
            direction.astype(jnp.bfloat16), leaf_blocks, bases, rank_weights
        )
        curvature = lax.psum(jnp.sum(direction * image_field, axis=1), "leaf")
        step_size = norm_now / curvature
        solution = solution + step_size[:, None] * direction
        residual = residual - step_size[:, None] * image_field
        if iteration + 1 < ITERS:
            norm_next = squares(residual)
            direction = residual + (norm_next / norm_now)[:, None] * direction
            norm_now = norm_next
    field_solution = jnp.zeros_like(solution).at[:, local_order].set(solution)
    field_residual = jnp.zeros_like(residual).at[:, local_order].set(residual)
    return (field_solution, field_residual)


def solution(mesh):
    return jax.shard_map(
        on_device,
        mesh=mesh,
        in_specs=(
            P("groups", "leaf"),
            P(("groups", "leaf")),
            P("leaf", None, None),
            P(None, None, "leaf"),
            P(),
        ),
        out_specs=(P("groups", "leaf"), P("groups", "leaf")),
        check_vma=False,
    )
```

profile of v0, /device:TPU:0, one launch (start us, length us, event | category | flops | bytes accessed | tf_op | source)
XLA Modules:
  0.0 227.0 jit_solution(16715418856772773228)
XLA Ops:
  0.6 0.7 compare_and_fusion
  1.4 1.9 copy.14
  3.3 14.2 %gather_fusion = f32[4096,128]{1,0:T(8,128)} fusion(f32[128,4096]{0,1:T(8,128)S(1)} %copy.14, s32[4096]{0:T(1024)S(1)} %broadcast_clamp_fusion), kind=kCustom, calls=%fused_computation | custom fusion | bytes 4210688 | tf_op jit(solution)/shard_map/jit(_take)/gather | solution.py:76
  17.5 1.9 copy.15
  19.4 5.5 %fusion.25 = f32[8,7,128,128]{3,2,1,0:T(8,128)S(1)} fusion(bf16[7,16,8,8,512]{4,3,2,1,0:T(8,128)(2,1)} %bitcast.155, f32[128,8,512]{2,0,1:T(8,128)S(1)} %copy.15, pred[8,512]{1,0:T(8,128)(4,1)S(1)} %broadcast_in_dim.46), kind=kOutput, calls=%fused_computation.41 | convolution fusion | flops 940048384 | bytes 13111296 | tf_op jit(solution)/shard_map/nbp,lrbp->blnr/dot_general | solution.py:43
  25.0 0.1 slice_reduce_fusion.1
  25.1 0.5 collective-permute-start
  25.6 0.1 slice_reduce_fusion.3
  25.7 0.8 copy-done
  26.6 2.1 multiply_reduce_fusion.3
  28.9 0.8 fusion.47
  30.1 3.0 %collective-permute-start.1 = (f32[3,128,128]{2,1,0:T(8,128)S(1)}, f32[3,128,128]{2,1,0:T(8,128)S(1)}, u32[]{:S(2)}, u32[]{:S(2)}) collective-permute-start(f32[3,128,128]{2,1,0:T(8,128)S(1)} %slice.122), channel_id=1, source_target_pairs={{0,2},{1,3},{2,0},{3,1},{4,6},{5,7},{6,4},{7,5},{8,10},{9,11},{10,... | collective-permute-start | bytes 589832 | tf_op jit(solution)/shard_map/ppermute | solution.py:12
  33.2 4.8 %collective-permute-done.1 = f32[3,128,128]{2,1,0:T(8,128)S(1)} collective-permute-done((f32[3,128,128]{2,1,0:T(8,128)S(1)}, f32[3,128,128]{2,1,0:T(8,128)S(1)}, u32[]{:S(2)}, u32[]{:S(2)}) %collective-permute-start.1) | collective-permute-done | bytes 196640 | tf_op jit(solution)/shard_map/ppermute | solution.py:12
  38.0 1.9 collective-permute-start.2
  39.9 3.2 %collective-permute-done.2 = f32[2,128,128]{2,1,0:T(8,128)S(1)} collective-permute-done((f32[2,128,128]{2,1,0:T(8,128)S(1)}, f32[2,128,128]{2,1,0:T(8,128)S(1)}, u32[]{:S(2)}, u32[]{:S(2)}) %collective-permute-start.2) | collective-permute-done | bytes 131104 | tf_op jit(solution)/shard_map/ppermute | solution.py:12
  43.1 2.9 %collective-permute-start.3 = (f32[1,128,128]{2,1,0:T(8,128)S(1)}, f32[1,128,128]{2,1,0:T(8,128)S(1)}, u32[]{:S(2)}, u32[]{:S(2)}) collective-permute-start(f32[1,128,128]{2,1,0:T(8,128)S(1)} %slice.126), channel_id=1, source_target_pairs={{0,8},{1,9},{2,10},{3,11},{4,12},{5,13},{6,14},{7,15},{8,0},{9,1},... | collective-permute-start | bytes 196616 | tf_op jit(solution)/shard_map/ppermute | solution.py:12
  46.0 2.3 %collective-permute-done.3 = f32[1,128,128]{2,1,0:T(8,128)S(1)} collective-permute-done((f32[1,128,128]{2,1,0:T(8,128)S(1)}, f32[1,128,128]{2,1,0:T(8,128)S(1)}, u32[]{:S(2)}, u32[]{:S(2)}) %collective-permute-start.3) | collective-permute-done | bytes 65568 | tf_op jit(solution)/shard_map/ppermute | solution.py:12
  48.5 2.8 %multiply_reduce_fusion.2 = (f32[128]{0:T(128)S(1)}, f32[128,8,512]{2,0,1:T(8,128)}) fusion(f32[128,8,512]{2,0,1:T(8,128)S(1)} %copy.15, pred[8,512]{1,0:T(8,128)(4,1)S(1)} %broadcast_in_dim.46, f32[8,128,512]{2,1,0:T(8,128)S(1)} %fusion.47, bf16[7,8,128,128]{3,2,0,1:T(8,128)(2,1)S(1)} %broadcast_dynamic-update-slice_fusion.5, ...), kind=kOutput, calls=%fused_computation.39 | convolution fusion | flops 941621120 | bytes 15471104 | tf_op jit(solution)/shard_map/lbnr,lrbp->nbp/dot_general | solution.py:62
  51.3 31.1 %all-reduce = (f32[128]{0:T(128)S(1)}, f32[128]{0:T(128)S(1)}) all-reduce(f32[128]{0:T(128)S(1)} %multiply_reduce_fusion.3, f32[128]{0:T(128)S(1)} %get-tuple-element.29), channel_id=1, replica_groups=mesh['groups'=2,'leaf'=16] {'leaf'}, use_global_device_ids=true, to_apply=%region_1.2 | all-reduce | flops 256 | bytes 2048 | tf_op jit(solution)/shard_map/psum | solution.py:69
  82.4 2.1 multiply_reduce_fusion.1
  84.5 29.7 %psum.30 = f32[128]{0:T(128)S(1)} all-reduce(f32[128]{0:T(128)S(1)} %multiply_reduce_fusion.1), channel_id=1, replica_groups=mesh['groups'=2,'leaf'=16] {'leaf'}, use_global_device_ids=true, to_apply=%region_9.10 | all-reduce | flops 128 | bytes 1024 | tf_op jit(solution)/shard_map/psum | solution.py:69
  114.2 2.2 multiply_add_fusion
  116.4 6.3 %fusion.28 = f32[8,7,128,128]{3,2,1,0:T(8,128)S(1)} fusion(bf16[7,16,8,8,512]{4,3,2,1,0:T(8,128)(2,1)} %bitcast.156, f32[128,8,512]{2,0,1:T(8,128)S(1)} %multiply_add_fusion), kind=kOutput, calls=%fused_computation.42 | convolution fusion | flops 940048384 | bytes 13107200 | tf_op jit(solution)/shard_map/nbp,lrbp->blnr/dot_general | solution.py:43
  122.7 0.1 slice_reduce_fusion
  122.8 0.1 slice_reduce_fusion.2
  122.9 2.0 copy-done.6
  124.8 2.0 fusion.45
  127.0 0.7 constant_dynamic-update-slice_fusion.3
  127.9 0.8 constant_dynamic-update-slice_fusion.2
  128.6 1.8 copy.20
  130.5 0.7 broadcast_dynamic-update-slice_fusion.4
  131.3 0.1 collective-permute-start.5
  131.4 0.7 broadcast_dynamic-update-slice_fusion.3
  132.1 6.6 %collective-permute-done.5 = f32[3,128,128]{2,1,0:T(8,128)S(1)} collective-permute-done((f32[3,128,128]{2,1,0:T(8,128)S(1)}, f32[3,128,128]{2,1,0:T(8,128)S(1)}, u32[]{:S(2)}, u32[]{:S(2)}) %collective-permute-start.5) | collective-permute-done | bytes 196640 | tf_op jit(solution)/shard_map/ppermute | solution.py:12
  138.7 0.1 collective-permute-start.6
  138.8 5.1 %collective-permute-done.6 = f32[2,128,128]{2,1,0:T(8,128)S(1)} collective-permute-done((f32[2,128,128]{2,1,0:T(8,128)S(1)}, f32[2,128,128]{2,1,0:T(8,128)S(1)}, u32[]{:S(2)}, u32[]{:S(2)}) %collective-permute-start.6) | collective-permute-done | bytes 131104 | tf_op jit(solution)/shard_map/ppermute | solution.py:12
  144.0 0.7 broadcast_dynamic-update-slice_fusion.2
  144.8 4.8 %collective-permute-done.7 = f32[1,128,128]{2,1,0:T(8,128)S(1)} collective-permute-done((f32[1,128,128]{2,1,0:T(8,128)S(1)}, f32[1,128,128]{2,1,0:T(8,128)S(1)}, u32[]{:S(2)}, u32[]{:S(2)}) %collective-permute-start.7) | collective-permute-done | bytes 65568 | tf_op jit(solution)/shard_map/ppermute | solution.py:12
  149.6 0.7 broadcast_dynamic-update-slice_fusion.1
  150.3 0.7 broadcast_dynamic-update-slice_fusion
  151.1 6.4 %multiply_reduce_fusion = (f32[128]{0:T(128)S(1)}, f32[128,8,512]{2,0,1:T(8,128)}) fusion(f32[128,8,512]{2,0,1:T(8,128)S(1)} %copy-done.3, f32[8,128,512]{2,1,0:T(8,128)S(1)} %copy-done.7, bf16[7,8,128,128]{3,2,0,1:T(8,128)(2,1)} %broadcast_dynamic-update-slice_fusion, bf16[7,16,8,8,512]{4,3,2,1,0:T(8,128)(2,1)} %bitcast.157), kind=kOutput, calls=%fused_computation.34 | convolution fusion | flops 941096832 | bytes 15467008 | tf_op jit(solution)/shard_map/lbnr,lrbp->nbp/dot_general | solution.py:62
  157.4 29.5 %psum.31 = f32[128]{0:T(128)S(1)} all-reduce(f32[128]{0:T(128)S(1)} %get-tuple-element.31), channel_id=1, replica_groups=mesh['groups'=2,'leaf'=16] {'leaf'}, use_global_device_ids=true, to_apply=%region_15.16 | all-reduce | flops 128 | bytes 1024 | tf_op jit(solution)/shard_map/psum | solution.py:85
  186.9 3.1 %copy.21 = f32[128,8,512]{0,2,1:T(8,128)} copy(f32[128,8,512]{2,0,1:T(8,128)} %get-tuple-element.32) | data formatting | bytes 4194304 | tf_op jit(solution)/shard_map/add | solution.py:65
  190.0 3.9 %fusion.14 = (f32[128,4096]{0,1:T(8,128)}, f32[128,4096]{0,1:T(8,128)}) fusion(f32[128,8,512]{0,2,1:T(8,128)} %copy.21, f32[128]{0:T(128)S(1)} %div.11, f32[128,8,512]{0,2,1:T(8,128)} %copy.20, f32[128]{0:T(128)S(1)} %div.9, f32[4096,128]{1,0:T(8,128)S(1)} %copy-done.1, pred[4096]{0:T(1024)(128)(4,1)S(1)} %get-tuple-element.10), kind=kLoop, calls=%fused_computation.20 | loop fusion | flops 2621440 | bytes 10490880 | tf_op jit(solution)/shard_map/sub | solution.py:88
  193.9 12.5 %scatter_custom_fusion.1 = f32[128,4096]{0,1:T(8,128)} fusion(s32[4096]{0:T(1024)S(1)} %get-tuple-element.11, f32[128,4096]{0,1:T(8,128)} %get-tuple-element.8, f32[]{:T(128)} %constant.13.clone.1), kind=kCustom, calls=%fused_computation.17 | custom fusion | bytes 4194308 | tf_op jit(solution)/shard_map/scatter | solution.py:94
  206.4 2.9 %copy.23 = f32[128,4096]{1,0:T(8,128)} copy(f32[128,4096]{0,1:T(8,128)} %scatter_custom_fusion.1) | data formatting | bytes 4194304
  209.3 14.8 %scatter_custom_fusion = f32[128,4096]{0,1:T(8,128)} fusion(s32[4096]{0:T(1024)S(1)} %get-tuple-element.11, f32[128,4096]{0,1:T(8,128)} %get-tuple-element.9, f32[4096,128]{1,0:T(8,128)S(1)} %copy-done.1, f32[128]{0:T(128)S(1)} %div.10, f32[128]{0:T(128)S(1)} %div.11, f32[128]{0:T(128)S(1)} %div.9, f32[]{:T(128)} %constant.18.clone.1, ...), kind=kCustom, calls=%fused_computation.21 | custom fusion | flops 3145728 | bytes 6297096 | tf_op jit(solution)/shard_map/scatter | solution.py:93
  224.1 2.9 %copy.22 = f32[128,4096]{1,0:T(8,128)} copy(f32[128,4096]{0,1:T(8,128)} %scatter_custom_fusion) | data formatting | bytes 4194304
  (70 shorter events, 1.2 us)
Async XLA Ops:
  25.0 1.6 copy-start
  25.1 3.6 %copy-start.8 = (f32[7,128]{1,0:T(8,128)S(1)}, f32[7,128]{1,0:T(8,128)}, u32[]{:S(2)}) copy-start(f32[7,128]{1,0:T(8,128)} %param.9) | copy-start | bytes 10756
  25.1 4.9 %collective-permute-start = (f32[4,128,128]{2,1,0:T(8,128)S(1)}, f32[4,128,128]{2,1,0:T(8,128)S(1)}, u32[]{:S(2)}, u32[]{:S(2)}) collective-permute-start(f32[4,128,128]{2,1,0:T(8,128)S(1)} %slice_reduce_fusion.1), channel_id=1, source_target_pairs={{0,1},{1,0},{2,3},{3,2},{4,5},{5,4},{6,7},{7,6},{8,9},{9,8},{10,11... | collective-permute-start | bytes 786440 | tf_op jit(solution)/shard_map/ppermute | solution.py:12
  26.6 2.4 %copy-start.5 = (bf16[8,512,512]{2,1,0:T(8,128)(2,1)S(1)}, bf16[8,512,512]{2,1,0:T(8,128)(2,1)}, u32[]{:S(2)}) copy-start(bf16[8,512,512]{2,1,0:T(8,128)(2,1)} %param.7) | copy-start | bytes 12582916
  28.9 19.6 %slice-start = ((s8[7340032]{0:T(1024)(128)(4,1)}), s8[4194304]{0:T(1024)(128)(4,1)S(1)}, s32[]{:S(2)}) async-start(s8[7340032]{0:T(1024)(128)(4,1)} %bitcast.158), calls=%async_computation | async-start | bytes 8388608
  28.9 19.6 %slice-start.1 = ((s8[7340032]{0:T(1024)(128)(4,1)}), s8[3145728]{0:T(1024)(128)(4,1)S(1)}, s32[]{:S(2)}) async-start(s8[7340032]{0:T(1024)(128)(4,1)} %bitcast.158), calls=%async_computation.1 | async-start | bytes 6291456
  30.1 7.9 %collective-permute-start.1 = (f32[3,128,128]{2,1,0:T(8,128)S(1)}, f32[3,128,128]{2,1,0:T(8,128)S(1)}, u32[]{:S(2)}, u32[]{:S(2)}) collective-permute-start(f32[3,128,128]{2,1,0:T(8,128)S(1)} %slice.122), channel_id=1, source_target_pairs={{0,2},{1,3},{2,0},{3,1},{4,6},{5,7},{6,4},{7,5},{8,10},{9,11},{10,... | collective-permute-start | bytes 589832 | tf_op jit(solution)/shard_map/ppermute | solution.py:12
  38.0 5.0 %collective-permute-start.2 = (f32[2,128,128]{2,1,0:T(8,128)S(1)}, f32[2,128,128]{2,1,0:T(8,128)S(1)}, u32[]{:S(2)}, u32[]{:S(2)}) collective-permute-start(f32[2,128,128]{2,1,0:T(8,128)S(1)} %slice.124), channel_id=1, source_target_pairs={{0,4},{1,5},{2,6},{3,7},{4,0},{5,1},{6,2},{7,3},{8,12},{9,13},{10,... | collective-permute-start | bytes 393224 | tf_op jit(solution)/shard_map/ppermute | solution.py:12
  43.1 5.2 %collective-permute-start.3 = (f32[1,128,128]{2,1,0:T(8,128)S(1)}, f32[1,128,128]{2,1,0:T(8,128)S(1)}, u32[]{:S(2)}, u32[]{:S(2)}) collective-permute-start(f32[1,128,128]{2,1,0:T(8,128)S(1)} %slice.126), channel_id=1, source_target_pairs={{0,8},{1,9},{2,10},{3,11},{4,12},{5,13},{6,14},{7,15},{8,0},{9,1},... | collective-permute-start | bytes 196616 | tf_op jit(solution)/shard_map/ppermute | solution.py:12
  116.4 6.5 %copy-start.2 = (f32[128,8,512]{2,0,1:T(8,128)}, f32[128,8,512]{2,0,1:T(8,128)S(1)}, u32[]{:S(2)}) copy-start(f32[128,8,512]{2,0,1:T(8,128)S(1)} %multiply_add_fusion) | copy-start | bytes 6291460
  122.7 2.2 copy-start.6
  126.9 1.7 copy-start.4
  126.9 4.3 %collective-permute-start.4 = (f32[4,128,128]{2,1,0:T(8,128)S(1)}, f32[4,128,128]{2,1,0:T(8,128)S(1)}, u32[]{:S(2)}, u32[]{:S(2)}) collective-permute-start(f32[4,128,128]{2,1,0:T(8,128)S(1)} %slice_reduce_fusion), channel_id=1, source_target_pairs={{0,1},{1,0},{2,3},{3,2},{4,5},{5,4},{6,7},{7,6},{8,9},{9,8},{10,11... | collective-permute-start | bytes 786440 | tf_op jit(solution)/shard_map/ppermute | solution.py:12
  131.2 19.9 %copy-start.3 = (f32[128,8,512]{2,0,1:T(8,128)S(1)}, f32[128,8,512]{2,0,1:T(8,128)}, u32[]{:S(2)}) copy-start(f32[128,8,512]{2,0,1:T(8,128)} %copy-done.2) | copy-start | bytes 6291460
  131.2 19.9 %copy-start.7 = (f32[8,128,512]{2,1,0:T(8,128)S(1)}, f32[8,128,512]{2,1,0:T(8,128)}, u32[]{:S(2)}) copy-start(f32[8,128,512]{2,1,0:T(8,128)} %fusion.45) | copy-start | bytes 6291460
  131.3 7.4 %collective-permute-start.5 = (f32[3,128,128]{2,1,0:T(8,128)S(1)}, f32[3,128,128]{2,1,0:T(8,128)S(1)}, u32[]{:S(2)}, u32[]{:S(2)}) collective-permute-start(f32[3,128,128]{2,1,0:T(8,128)S(1)} %slice.132), channel_id=1, source_target_pairs={{0,2},{1,3},{2,0},{3,1},{4,6},{5,7},{6,4},{7,5},{8,10},{9,11},{10,... | collective-permute-start | bytes 589832 | tf_op jit(solution)/shard_map/ppermute | solution.py:12
  138.7 5.2 %collective-permute-start.6 = (f32[2,128,128]{2,1,0:T(8,128)S(1)}, f32[2,128,128]{2,1,0:T(8,128)S(1)}, u32[]{:S(2)}, u32[]{:S(2)}) collective-permute-start(f32[2,128,128]{2,1,0:T(8,128)S(1)} %slice.134), channel_id=1, source_target_pairs={{0,4},{1,5},{2,6},{3,7},{4,0},{5,1},{6,2},{7,3},{8,12},{9,13},{10,... | collective-permute-start | bytes 393224 | tf_op jit(solution)/shard_map/ppermute | solution.py:12
  143.9 5.7 %collective-permute-start.7 = (f32[1,128,128]{2,1,0:T(8,128)S(1)}, f32[1,128,128]{2,1,0:T(8,128)S(1)}, u32[]{:S(2)}, u32[]{:S(2)}) collective-permute-start(f32[1,128,128]{2,1,0:T(8,128)S(1)} %slice.136), channel_id=1, source_target_pairs={{0,8},{1,9},{2,10},{3,11},{4,12},{5,13},{6,14},{7,15},{8,0},{9,1},... | collective-permute-start | bytes 196616 | tf_op jit(solution)/shard_map/ppermute | solution.py:12
  186.9 3.1 %copy-start.1 = (f32[4096,128]{1,0:T(8,128)S(1)}, f32[4096,128]{1,0:T(8,128)}, u32[]{:S(2)}) copy-start(f32[4096,128]{1,0:T(8,128)} %gather_fusion) | copy-start | bytes 6291460
where the time goes:
time: 228 us; the launch traced here: 227 us
  blocking collectives  90.2 us (40%)
  local copies, waits for them, and re-layouts  49.9 us (22%)
  waiting for transfers between devices  26.8 us (12%)
  other arithmetic  26.7 us (12%)
  matrix products  23.8 us (10%)
  starting transfers between devices  8.49 us (4%)
    psum x2, blocking collectives, squares(): return lax.psum(jnp.sum(values * values, axis=1), 'leaf')  60.8 us
    psum x1, blocking collectives, on_device(): curvature = lax.psum(jnp.sum(direction * image_field, axis=1), 'leaf')  29.5 us
    ppermute x8, waiting for transfers between devices, from_partner(): lax.ppermute(array, axis, [(i, i ^ 1 << stride) for i in range(lax.axis_s...  26.8 us
    gather x2, local copies, waits for them, and re-layouts, on_device(): ordered = jnp.take(right_side, local_order, axis=1)  16.1 us
    unnamed x37, local copies, waits for them, and re-layouts  15.3 us
    scatter x1, other arithmetic, on_device(): field_solution = jnp.zeros_like(solution).at[:, local_order].set(solution)  14.8 us
    scatter x1, local copies, waits for them, and re-layouts, on_device(): field_residual = jnp.zeros_like(residual).at[:, local_order].set(residual)  12.5 us
    dot_general x2, matrix products, apply_operator(): jnp.einsum('nbp,lrbp->blnr', probe_tiles, basis_tiles, preferred_element_...  11.8 us
  transfers between devices with their start and end apart: 8, of which 6 were waited for; matrix products, arithmetic and copies ran while one was open for 4% of the time, Pallas kernels for 0%

commit v1 on v0

v1 whole, which is shorter than its diff:
```python
import functools
import math

import jax
import jax.numpy as jnp
from jax import lax
from jax.experimental import pallas as pl
from jax.experimental.pallas import tpu as pltpu
from jax.sharding import PartitionSpec as P

ITERS = 2
TILE = 128
MESH = pl.DeviceIdType.MESH


def nt_dot(a, b):
    return lax.dot_general(a, b, (((1,), (1,)), ((), ())), preferred_element_type=jnp.float32)


def nn_dot(a, b):
    return jnp.dot(a, b, preferred_element_type=jnp.float32)


def row_of(matrix):
    return jnp.sum(matrix.T, axis=0, keepdims=True)


def spread(row):
    return jnp.broadcast_to(row, (TILE, row.shape[1])).T


def cg_kernel(n_dev, levels, *refs):
    upper = n_dev.bit_length() - 1
    local = levels - upper
    rs_hbm, order_ref, leaf_hbm, bases_hbm, weights_ref, sol_ref, res_ref = refs[:7]
    (rs, rst, rows, leaf, bases, dirn, probe, image, coef, low_s, up_s, pend0, recv_a, recv_b, total,
     vec_out, vec_in) = refs[7:24]
    pends = refs[24:24 + upper - 1]
    recvs = refs[24 + upper - 1:24 + 2 * (upper - 1)]
    rs_sem, leaf_sem, bases_sem, send_sem, recv_sem, vsend_sem, vrecv_sem = refs[24 + 2 * (upper - 1):]

    columns, points = rs.shape
    blocks, leaf_size = leaf.shape[0], leaf.shape[1]
    tiles = points // TILE
    half = columns // 2
    me = lax.axis_index("leaf")
    core = me % 2

    rs_copy = pltpu.make_async_copy(rs_hbm, rs, rs_sem)
    rs_copy.start()
    bases_copy = pltpu.make_async_copy(bases_hbm, bases, bases_sem)
    bases_copy.start()
    leaf_copy = pltpu.make_async_copy(leaf_hbm, leaf, leaf_sem)
    leaf_copy.start()

    barrier = pltpu.get_barrier_semaphore()

    def greet(k, carry):
        pl.semaphore_signal(
            barrier, inc=1, device_id={"leaf": (me + k) % n_dev}, device_id_type=MESH
        )
        return carry

    lax.fori_loop(1, n_dev, greet, 0)

    rs_copy.wait()

    def turn(c, carry):
        at = pl.multiple_of(c * TILE, TILE)
        rst[pl.ds(at, TILE), :] = rs[:, pl.ds(at, TILE)].T
        return carry

    lax.fori_loop(0, tiles, turn, 0)

    def fetch(c, carry):
        at = pl.multiple_of(c * TILE, TILE)
        for j in range(TILE):
            source = order_ref[at + j] & (points - 1)
            rows[pl.ds(j, 1), :] = rst[pl.ds(source, 1), :]
        picked = rows[...].T
        dirn[:, pl.ds(at, TILE)] = picked
        probe[:, pl.ds(at, TILE)] = picked.astype(jnp.bfloat16)
        return carry

    lax.fori_loop(0, tiles, fetch, 0)

    def partner(bit):
        stride = 2 ** bit
        return me + stride * (1 - 2 * ((me // stride) % 2))

    def send(source, target, it, slot, bit):
        copy = pltpu.make_async_remote_copy(
            src_ref=source,
            dst_ref=target,
            send_sem=send_sem.at[it, slot],
            recv_sem=recv_sem.at[it, slot],
            device_id={"leaf": partner(bit)},
            device_id_type=MESH,
        )
        copy.start()
        return copy

    def scaled(values, level):
        factor = 1.0 / math.sqrt(columns_rank * leaf_size * 2 ** (level + 1))
        return (values * factor * weights_ref[level:level + 1, :]).astype(jnp.bfloat16)

    columns_rank = weights_ref.shape[1]
    rank = columns_rank
    mine = pl.ds(pl.multiple_of(core * half, half), half)
    theirs = pl.ds(pl.multiple_of((1 - core) * half, half), half)
    low = local * rank
    bases_copy.wait()

    for it in range(ITERS):
        up = nt_dot(probe[...], bases[low:, :])
        for u in range(upper):
            pend0[it, u] = up[:, u * rank:(u + 1) * rank]
        if it == 0:
            pl.semaphore_wait(barrier, n_dev - 1)
        whole_copy = send(pend0.at[it, 0], recv_a.at[it], it, 0, 0)
        half_copy = send(pend0.at[it, pl.ds(1, upper - 1), theirs], recv_b.at[it], it, 1, 0)
        sent = [whole_copy, half_copy]
        back = []
        state = {"round": 0, "copy": None}

        def advance():
            t = state["round"]
            if t >= upper:
                return
            if t == 0:
                whole_copy.wait_recv()
                half_copy.wait_recv()
                total[it, 0] = pend0[it, 0] + recv_a[it]
                pends[0][it] = pend0[it, pl.ds(1, upper - 1), mine] + recv_b[it]
            else:
                state["copy"].wait_recv()
                total[it, t, mine] = pends[t - 1][it, 0] + recvs[t - 1][it, 0]
                gather = send(total.at[it, t, mine], total.at[it, t, mine], it, upper + t, 0)
                back.append(gather)
                sent.append(gather)
                if t + 1 < upper:
                    pends[t][it] = pends[t - 1][it, 1:] + recvs[t - 1][it, 1:]
            if t + 1 < upper:
                state["copy"] = send(pends[t].at[it], recvs[t].at[it], it, 2 + t, t + 1)
                sent.append(state["copy"])
            state["round"] = t + 1

        for b in range(blocks):
            span = slice(b * leaf_size, (b + 1) * leaf_size)
            coef[b] = nt_dot(probe[:, span], bases[:low, span])
        for level in range(local):
            per_node = 2 ** (level + 1)
            lanes = slice(level * rank, (level + 1) * rank)
            for q in range(blocks // per_node):
                node = coef[q * per_node, :, lanes]
                for b in range(q * per_node + 1, (q + 1) * per_node):
                    node = node + coef[b, :, lanes]
                value = scaled(node, level)
                for b in range(q * per_node, (q + 1) * per_node):
                    low_s[b, :, lanes] = value
        advance()
        if it == 0:
            leaf_copy.wait()
        for b in range(blocks):
            span = slice(b * leaf_size, (b + 1) * leaf_size)
            image[:, span] = nn_dot(probe[:, span], leaf[b]) + nn_dot(low_s[b], bases[:low, span])
            if b % 4 == 3:
                advance()
        for _ in range(upper):
            advance()
        for copy in back:
            copy.wait_recv()
        for u in range(upper):
            up_s[:, u * rank:(u + 1) * rank] = scaled(total[it, u], local + u)

        curve = jnp.zeros((columns, TILE), jnp.float32)
        norm = jnp.zeros((columns, TILE), jnp.float32)
        power = jnp.zeros((columns, TILE), jnp.float32)
        held = dirn if it == 0 else res_ref
        for b in range(blocks):
            span = slice(b * leaf_size, (b + 1) * leaf_size)
            field = image[:, span] + nn_dot(up_s[...], bases[low:, span])
            image[:, span] = field
            for c in range(leaf_size // TILE):
                at = b * leaf_size + c * TILE
                piece = field[:, c * TILE:(c + 1) * TILE]
                away = dirn[:, at:at + TILE]
                curve = curve + away * piece
                left = held[:, at:at + TILE]
                norm = norm + left * left
                if it + 1 < ITERS:
                    power = power + piece * piece
        vec_out[it, 0:1, :] = row_of(curve)
        vec_out[it, 1:2, :] = row_of(norm)
        vec_out[it, 2:3, :] = row_of(power)
        vec_out[it, 3:8, :] = jnp.zeros((5, TILE), jnp.float32)

        def vector(k):
            return pltpu.make_async_remote_copy(
                src_ref=vec_out.at[it],
                dst_ref=vec_in.at[it, k],
                send_sem=vsend_sem.at[it, k],
                recv_sem=vrecv_sem.at[it, k],
                device_id={"leaf": (me + k) % n_dev},
                device_id_type=MESH,
            )

        def push(k, carry):
            vector(k).start()
            return carry

        def take(k, carry):
            vector(k).wait()
            return carry + vec_in[it, k]

        lax.fori_loop(1, n_dev, push, 0)
        for copy in sent:
            copy.wait_send()
        sums = lax.fori_loop(1, n_dev, take, vec_out[it])
        curvature, norm_now, squares = sums[0:1], sums[1:2], sums[2:3]
        step_row = norm_now / curvature
        step = spread(step_row)
        if it + 1 < ITERS:
            norm_next = norm_now - 2.0 * step_row * curvature + step_row * step_row * squares
            ratio = spread(norm_next / norm_now)

        def update(c, carry):
            lanes = pl.ds(pl.multiple_of(c * TILE, TILE), TILE)
            away = dirn[:, lanes]
            if it == 0:
                sol_ref[:, lanes] = step * away
                left = away - step * image[:, lanes]
            else:
                sol_ref[:, lanes] = sol_ref[:, lanes] + step * away
                left = res_ref[:, lanes] - step * image[:, lanes]
            res_ref[:, lanes] = left
            if it + 1 < ITERS:
                fresh = left + ratio * away
                dirn[:, lanes] = fresh
                probe[:, lanes] = fresh.astype(jnp.bfloat16)
            return carry

        lax.fori_loop(0, tiles, update, 0)


def conjugate(right_side, point_order, leaf_blocks, bases, rank_weights, n_dev):
    columns, points = right_side.shape
    blocks, leaf_size, _ = leaf_blocks.shape
    levels, rank = rank_weights.shape
    upper = n_dev.bit_length() - 1
    local = levels - upper
    half = columns // 2
    f32, bf16 = jnp.float32, jnp.bfloat16
    scratch = [
        pltpu.VMEM((columns, points), f32),
        pltpu.VMEM((points, columns), f32),
        pltpu.VMEM((TILE, columns), f32),
        pltpu.VMEM((blocks, leaf_size, leaf_size), bf16),
        pltpu.VMEM((levels * rank, points), bf16),
        pltpu.VMEM((columns, points), f32),
        pltpu.VMEM((columns, points), bf16),
        pltpu.VMEM((columns, points), f32),
        pltpu.VMEM((blocks, columns, local * rank), f32),
        pltpu.VMEM((blocks, columns, local * rank), bf16),
        pltpu.VMEM((columns, upper * rank), bf16),
        pltpu.VMEM((ITERS, upper, columns, rank), f32),
        pltpu.VMEM((ITERS, columns, rank), f32),
        pltpu.VMEM((ITERS, upper - 1, half, rank), f32),
        pltpu.VMEM((ITERS, upper, columns, rank), f32),
        pltpu.VMEM((ITERS, 8, columns), f32),
        pltpu.VMEM((ITERS, n_dev, 8, columns), f32),
    ]
    rounds = [pltpu.VMEM((ITERS, upper - t, half, rank), f32) for t in range(1, upper)]
    scratch += rounds + rounds
    scratch += [
        pltpu.SemaphoreType.DMA,
        pltpu.SemaphoreType.DMA,
        pltpu.SemaphoreType.DMA,
        pltpu.SemaphoreType.DMA((ITERS, 2 * upper)),
        pltpu.SemaphoreType.DMA((ITERS, 2 * upper)),
        pltpu.SemaphoreType.DMA((ITERS, n_dev)),
        pltpu.SemaphoreType.DMA((ITERS, n_dev)),
    ]
    hbm = pl.BlockSpec(memory_space=pl.ANY)
    vmem = pl.BlockSpec(memory_space=pltpu.VMEM)
    shape = jax.ShapeDtypeStruct((columns, points), f32)
    return pl.pallas_call(
        functools.partial(cg_kernel, n_dev, levels),
        out_shape=(shape, shape),
        in_specs=[hbm, pl.BlockSpec(memory_space=pltpu.SMEM), hbm, hbm, vmem],
        out_specs=(vmem, vmem),
        scratch_shapes=scratch,
        compiler_params=pltpu.CompilerParams(
            collective_id=0, has_side_effects=True, vmem_limit_bytes=56 * 2 ** 20
        ),
        name="cg",
    )(right_side, point_order, leaf_blocks, bases.reshape(levels * rank, points), rank_weights)


def scatter_kernel(order_ref, sol_ref, res_ref, out_sol, out_res, sol_rows, res_rows, sol_tile, res_tile):
    columns, points = sol_ref.shape
    tiles = points // TILE

    def place(c, carry):
        at = pl.multiple_of(c * TILE, TILE)
        sol_tile[...] = sol_ref[:, pl.ds(at, TILE)].T
        res_tile[...] = res_ref[:, pl.ds(at, TILE)].T
        for j in range(TILE):
            target = order_ref[at + j] & (points - 1)
            sol_rows[pl.ds(target, 1), :] = sol_tile[pl.ds(j, 1), :]
            res_rows[pl.ds(target, 1), :] = res_tile[pl.ds(j, 1), :]
        return carry

    lax.fori_loop(0, tiles, place, 0)

    def turn(c, carry):
        at = pl.multiple_of(c * TILE, TILE)
        out_sol[:, pl.ds(at, TILE)] = sol_rows[pl.ds(at, TILE), :].T
        out_res[:, pl.ds(at, TILE)] = res_rows[pl.ds(at, TILE), :].T
        return carry

    lax.fori_loop(0, tiles, turn, 0)


def scatter_back(point_order, field, residual):
    columns, points = field.shape
    vmem = pl.BlockSpec(memory_space=pltpu.VMEM)
    shape = jax.ShapeDtypeStruct((columns, points), jnp.float32)
    return pl.pallas_call(
        scatter_kernel,
        out_shape=(shape, shape),
        in_specs=[pl.BlockSpec(memory_space=pltpu.SMEM), vmem, vmem],
        out_specs=(vmem, vmem),
        scratch_shapes=[
            pltpu.VMEM((points, columns), jnp.float32),
            pltpu.VMEM((points, columns), jnp.float32),
            pltpu.VMEM((TILE, columns), jnp.float32),
            pltpu.VMEM((TILE, columns), jnp.float32),
        ],
        compiler_params=pltpu.CompilerParams(vmem_limit_bytes=40 * 2 ** 20),
        name="place",
    )(point_order, field, residual)


def on_device(right_side, point_order, leaf_blocks, bases, rank_weights, n_dev):
    field, residual = conjugate(right_side, point_order, leaf_blocks, bases, rank_weights, n_dev)
    return scatter_back(point_order, field, residual)


def solution(mesh):
    return jax.shard_map(
        functools.partial(on_device, n_dev=mesh.shape["leaf"]),
        mesh=mesh,
        in_specs=(
            P("groups", "leaf"),
            P(("groups", "leaf")),
            P("leaf", None, None),
            P(None, None, "leaf"),
            P(),
        ),
        out_specs=(P("groups", "leaf"), P("groups", "leaf")),
        check_vma=False,
    )
```

time: 228 us -> 76.5 us (0.34)
  blocking collectives: 90.2 us -> 0 us
  Pallas kernels: 0 us -> 72.4 us
  local copies, waits for them, and re-layouts: 49.9 us -> 3.18 us
  waiting for transfers between devices: 26.8 us -> 0 us
  other arithmetic: 26.7 us -> 0 us
  matrix products: 23.8 us -> 0 us
  starting transfers between devices: 8.49 us -> 0 us
    psum x3 -> x0, blocking collectives: 90.2 us -> none  [the longest x2 60.8 us: squares(): return lax.psum(jnp.sum(values * values, axis=1), 'leaf')]
    pallas_call x0 -> x2, Pallas kernels: none -> 72.4 us  [the longest x1 58.6 us: conjugate(): pl.pallas_call(functools.partial(cg_kernel, n_dev, levels), out_shape=(sh...]
    ppermute x8 -> x0, waiting for transfers between devices: 26.8 us -> none  [from_partner(): lax.ppermute(array, axis, [(i, i ^ 1 << stride) for i in range(lax.axis_s...]
    dot_general x6 -> x0, matrix products: 23.8 us -> none  [the longest x2 11.8 us: apply_operator(): jnp.einsum('nbp,lrbp->blnr', probe_tiles, basis_tiles, preferred_element_...]
    gather x2 -> x0, local copies, waits for them, and re-layouts: 16.1 us -> none  [on_device(): ordered = jnp.take(right_side, local_order, axis=1)]
    scatter x1 -> x0, other arithmetic: 14.8 us -> none  [on_device(): field_solution = jnp.zeros_like(solution).at[:, local_order].set(solution)]
    scatter x1 -> x0, local copies, waits for them, and re-layouts: 12.5 us -> none  [on_device(): field_residual = jnp.zeros_like(residual).at[:, local_order].set(residual)]
    unnamed x37 -> x6, local copies, waits for them, and re-layouts: 15.3 us -> 3.18 us
  transfers between devices with their start and end apart: 8 -> 0, of which waited for: 6 -> 0; matrix products, arithmetic and copies ran while one was open for 4% -> 0% of each run, Pallas kernels for 0% -> 0%
where the time goes in v1:
time: 76.5 us; the launch traced here: 76.2 us
  Pallas kernels  72.4 us (95%)
  local copies, waits for them, and re-layouts  3.18 us (4%)
    pallas_call x1, Pallas kernels, conjugate(): pl.pallas_call(functools.partial(cg_kernel, n_dev, levels), out_shape=(sh...  58.6 us
    pallas_call x1, Pallas kernels, scatter_back(): pl.pallas_call(scatter_kernel, out_shape=(shape, shape), in_specs=[pl.Blo...  13.8 us
    unnamed x6, local copies, waits for them, and re-layouts  3.18 us

profile of v1, /device:TPU:0, one launch (start us, length us, event | category | flops | bytes accessed | tf_op | source)
XLA Modules:
  0.0 76.2 jit_solution(18251518337031860849)
XLA Ops:
  0.6 0.0 copy-start.2
  0.6 58.6 %cg.1 = (f32[128,4096]{1,0:T(8,128)}, f32[128,4096]{1,0:T(8,128)}) custom-call(f32[128,4096]{1,0:T(8,128)} %refs_0_.1, s32[4096]{0:T(1024)} %order_ref.1, bf16[8,512,512]{2,1,0:T(8,128)(2,1)} %refs_2_.1, bf16[896,4096]{1,0:T(8,128)(2,1)} %bitcast.1, f32[7,128]{1,0:T(8,128)} %refs_4_.1), custom_call_target="tpu_custom_call" | custom-call | tf_op jit(solution)/shard_map/cg/pallas_call | solution.py:287
  59.2 0.0 copy-done.2
  59.2 0.0 copy-start
  59.3 1.6 %copy-done = f32[128,4096]{1,0:T(8,128)S(1)} copy-done((f32[128,4096]{1,0:T(8,128)S(1)}, f32[128,4096]{1,0:T(8,128)}, u32[]{:S(2)}) %copy-start) | copy-done | bytes 2097176
  60.8 0.0 copy-start.1
  60.8 1.6 %copy-done.1 = f32[128,4096]{1,0:T(8,128)S(1)} copy-done((f32[128,4096]{1,0:T(8,128)S(1)}, f32[128,4096]{1,0:T(8,128)}, u32[]{:S(2)}) %copy-start.1) | copy-done | bytes 2097176
  62.4 13.8 %place.1 = (f32[128,4096]{1,0:T(8,128)}, f32[128,4096]{1,0:T(8,128)}) custom-call(s32[4096]{0:T(1024)S(1)} %copy-done.2, f32[128,4096]{1,0:T(8,128)S(1)} %copy-done, f32[128,4096]{1,0:T(8,128)S(1)} %copy-done.1), custom_call_target="tpu_custom_call" | custom-call | tf_op jit(solution)/shard_map/place/pallas_call | solution.py:329
Async XLA Ops:
  0.6 58.6 %copy-start.2 = (s32[4096]{0:T(1024)S(1)}, s32[4096]{0:T(1024)}, u32[]{:S(2)}) copy-start(s32[4096]{0:T(1024)} %order_ref.1) | copy-start | bytes 49156
  59.2 1.6 %copy-start = (f32[128,4096]{1,0:T(8,128)S(1)}, f32[128,4096]{1,0:T(8,128)}, u32[]{:S(2)}) copy-start(f32[128,4096]{1,0:T(8,128)} %get-tuple-element.4.sol_ref) | copy-start | bytes 6291460
  60.8 1.6 %copy-start.1 = (f32[128,4096]{1,0:T(8,128)S(1)}, f32[128,4096]{1,0:T(8,128)}, u32[]{:S(2)}) copy-start(f32[128,4096]{1,0:T(8,128)} %get-tuple-element.5.res_ref) | copy-start | bytes 6291460

commit v2 on v1

v2 whole, which is shorter than its diff:
```python
import functools
import math

import jax
import jax.numpy as jnp
from jax import lax
from jax.experimental import pallas as pl
from jax.experimental.pallas import tpu as pltpu
from jax.sharding import PartitionSpec as P

ITERS = 2
TILE = 128
CHUNKS = 4
MESH = pl.DeviceIdType.MESH


def nt_dot(a, b):
    return lax.dot_general(a, b, (((1,), (1,)), ((), ())), preferred_element_type=jnp.float32)


def nn_dot(a, b):
    return jnp.dot(a, b, preferred_element_type=jnp.float32)


def row_of(matrix):
    return jnp.sum(matrix.T, axis=0, keepdims=True)


def spread(row):
    return jnp.broadcast_to(row, (TILE, row.shape[1])).T


def cg_kernel(n_dev, levels, n_stage, *refs):
    upper = n_dev.bit_length() - 1
    local = levels - upper
    refs = list(refs)

    def grab(count):
        taken = refs[:count]
        del refs[:count]
        return taken

    rs_hbm, order_ref, leaf_hbm, bases_hbm, weights_ref, sol_hbm, res_hbm = grab(7)
    rs, rst, rows, srows, leaf, bases, dirn, left_field, probe, image, coef, low_s, up_s = grab(13)
    pend0, recv_a, recv_q, total, vec_out, vec_in = grab(6)
    pends, firsts, others = grab(n_stage), grab(n_stage), grab(n_stage)
    rs_sem, leaf_sem, bases_sem, send_sem, recv_sem, vsend_sem, vrecv_sem, out_sem = grab(8)

    columns, points = rs.shape
    blocks, leaf_size = leaf.shape[0], leaf.shape[1]
    rank = weights_ref.shape[1]
    tiles = points // TILE
    quarter = columns // 4
    me = lax.axis_index("leaf")

    part = points // CHUNKS
    rs_copies = []
    for q in range(CHUNKS):
        lanes = pl.ds(q * part, part)
        copy = pltpu.make_async_copy(rs_hbm.at[:, lanes], rs.at[:, lanes], rs_sem.at[q])
        copy.start()
        rs_copies.append(copy)
    bases_copy = pltpu.make_async_copy(bases_hbm, bases, bases_sem)
    bases_copy.start()
    leaf_copy = pltpu.make_async_copy(leaf_hbm, leaf, leaf_sem)
    leaf_copy.start()

    barrier = pltpu.get_barrier_semaphore()

    def greet(k, carry):
        pl.semaphore_signal(
            barrier, inc=1, device_id={"leaf": (me + k) % n_dev}, device_id_type=MESH
        )
        return carry

    lax.fori_loop(1, n_dev, greet, 0)

    for q in range(CHUNKS):
        rs_copies[q].wait()
        for c in range(q * tiles // CHUNKS, (q + 1) * tiles // CHUNKS):
            at = c * TILE
            rst[at:at + TILE, :] = rs[:, at:at + TILE].T

    def fetch(at):
        for j in range(TILE):
            source = order_ref[at + j] & (points - 1)
            rows[pl.ds(j, 1), :] = rst[pl.ds(source, 1), :]

    def keep(at, tile):
        picked = tile.T
        dirn[:, pl.ds(at, TILE)] = picked
        probe[:, pl.ds(at, TILE)] = picked.astype(jnp.bfloat16)

    def fetch_keep(c, carry):
        at = pl.multiple_of(c * TILE, TILE)
        before = rows[...]
        fetch(at)
        keep(pl.multiple_of(at - TILE, TILE), before)
        return carry

    fetch(0)
    lax.fori_loop(1, tiles, fetch_keep, 0)
    keep(points - TILE, rows[...])

    def flip(k, bit):
        peer = me
        for step in range(2):
            if k >> step & 1:
                stride = 2 ** (bit + step)
                peer = peer + stride * (1 - 2 * ((me // stride) % 2))
        return peer

    def quarter_of(device):
        return pl.ds(pl.multiple_of(device % 4 * quarter, quarter), quarter)

    def scaled(values, level):
        factor = 1.0 / math.sqrt(rank * leaf_size * 2 ** (level + 1))
        return (values * factor * weights_ref[level:level + 1, :]).astype(jnp.bfloat16)

    mine = quarter_of(me)
    low = local * rank
    bases_copy.wait()

    for it in range(ITERS):
        up = nt_dot(probe[...], bases[low:, :])
        for u in range(upper):
            pend0[it, u] = up[:, u * rank:(u + 1) * rank]
        if it == 0:
            pl.semaphore_wait(barrier, n_dev - 1)
        sent = []

        def send(source, target, k, bit):
            slot = len(sent)
            copy = pltpu.make_async_remote_copy(
                src_ref=source,
                dst_ref=target,
                send_sem=send_sem.at[it, slot],
                recv_sem=recv_sem.at[it, slot],
                device_id={"leaf": flip(k, bit)},
                device_id_type=MESH,
            )
            copy.start()
            sent.append(copy)
            return copy

        def share(first, count):
            place = total.at[it, pl.ds(first, count), mine]
            return [send(place, place, k, 0) for k in (3, 2, 1)]

        def launch(stage):
            bit = 2 * stage + 2
            count = upper - bit
            copies = [send(pends[stage].at[it], firsts[stage].at[it], 1, bit)]
            if count > 1:
                for k in (2, 3):
                    copies.append(send(
                        pends[stage].at[it, pl.ds(1, count - 1)],
                        others[stage].at[it, k - 2], k, bit))
            return copies

        opening = [
            send(pend0.at[it, pl.ds(1, upper - 1), quarter_of(flip(k, 0))],
                 recv_q.at[it, k - 1], k, 0)
            for k in (3, 2, 1)
        ]
        opening.append(send(pend0.at[it, 0], recv_a.at[it], 1, 0))
        state = {"round": 0, "copies": opening, "back": []}

        def advance():
            stage = state["round"] - 1
            if stage >= n_stage:
                return
            for copy in state["copies"]:
                copy.wait_recv()
            if stage < 0:
                for u in range(1, upper):
                    value = pend0[it, u, mine]
                    for k in range(3):
                        value = value + recv_q[it, k, u - 1]
                    if u == 1:
                        total[it, u, mine] = value
                    else:
                        pends[0][it, u - 2] = value
                if n_stage > 0:
                    state["copies"] = launch(0)
                state["back"] += share(1, 1)
                total[it, 0] = pend0[it, 0] + recv_a[it]
            else:
                bit = 2 * stage + 2
                for u in range(bit, upper):
                    value = pends[stage][it, u - bit] + firsts[stage][it, u - bit]
                    if u > bit:
                        for k in range(2):
                            value = value + others[stage][it, k, u - bit - 1]
                    if u < bit + 2:
                        total[it, u, mine] = value
                    else:
                        pends[stage + 1][it, u - bit - 2] = value
                if stage + 1 < n_stage:
                    state["copies"] = launch(stage + 1)
                state["back"] += share(bit, min(2, upper - bit))
            state["round"] += 1

        for b in range(blocks):
            span = slice(b * leaf_size, (b + 1) * leaf_size)
            coef[b] = nt_dot(probe[:, span], bases[:low, span])
        for level in range(local):
            per_node = 2 ** (level + 1)
            lanes = slice(level * rank, (level + 1) * rank)
            for q in range(blocks // per_node):
                node = coef[q * per_node, :, lanes]
                for b in range(q * per_node + 1, (q + 1) * per_node):
                    node = node + coef[b, :, lanes]
                value = scaled(node, level)
                for b in range(q * per_node, (q + 1) * per_node):
                    low_s[b, :, lanes] = value
        if it == 0:
            leaf_copy.wait()
        for b in range(blocks):
            span = slice(b * leaf_size, (b + 1) * leaf_size)
            image[:, span] = nn_dot(probe[:, span], leaf[b]) + nn_dot(low_s[b], bases[:low, span])
            if b == blocks - 3:
                advance()
        for _ in range(n_stage):
            advance()
        for copy in state["back"]:
            copy.wait_recv()
        for u in range(upper):
            up_s[:, u * rank:(u + 1) * rank] = scaled(total[it, u], local + u)

        curve = jnp.zeros((columns, TILE), jnp.float32)
        norm = jnp.zeros((columns, TILE), jnp.float32)
        power = jnp.zeros((columns, TILE), jnp.float32)
        held = dirn if it == 0 else left_field
        for b in range(blocks):
            span = slice(b * leaf_size, (b + 1) * leaf_size)
            field = image[:, span] + nn_dot(up_s[...], bases[low:, span])
            image[:, span] = field
            for c in range(leaf_size // TILE):
                at = b * leaf_size + c * TILE
                piece = field[:, c * TILE:(c + 1) * TILE]
                away = dirn[:, at:at + TILE]
                curve = curve + away * piece
                left = held[:, at:at + TILE]
                norm = norm + left * left
                if it + 1 < ITERS:
                    power = power + piece * piece
        vec_out[it, 0, 0:1, :] = row_of(curve)
        vec_out[it, 0, 1:2, :] = row_of(norm)
        vec_out[it, 0, 2:3, :] = row_of(power)
        vec_out[it, 0, 3:8, :] = jnp.zeros((5, TILE), jnp.float32)
        for stage in range(n_stage + 1):
            bit = 2 * stage
            peers = (3, 2, 1) if bit + 1 < upper else (1,)
            hops = []
            for k in peers:
                slot = stage * 3 + k - 1
                hop = pltpu.make_async_remote_copy(
                    src_ref=vec_out.at[it, stage],
                    dst_ref=vec_in.at[it, slot],
                    send_sem=vsend_sem.at[it, slot],
                    recv_sem=vrecv_sem.at[it, slot],
                    device_id={"leaf": flip(k, bit)},
                    device_id_type=MESH,
                )
                hop.start()
                hops.append(hop)
            if stage == 0:
                for copy in sent:
                    copy.wait_send()
            sums = vec_out[it, stage]
            for hop, k in zip(hops, peers):
                hop.wait()
                sums = sums + vec_in[it, stage * 3 + k - 1]
            if stage < n_stage:
                vec_out[it, stage + 1] = sums
        curvature, norm_now, squares = sums[0:1], sums[1:2], sums[2:3]
        step_row = norm_now / curvature
        step = spread(step_row)
        if it + 1 < ITERS:
            norm_next = norm_now - 2.0 * step_row * curvature + step_row * step_row * squares
            ratio = spread(norm_next / norm_now)
            for c in range(tiles):
                lanes = slice(c * TILE, (c + 1) * TILE)
                away = dirn[:, lanes]
                if it == 0:
                    rs[:, lanes] = step * away
                    left = away - step * image[:, lanes]
                else:
                    rs[:, lanes] = rs[:, lanes] + step * away
                    left = left_field[:, lanes] - step * image[:, lanes]
                left_field[:, lanes] = left
                fresh = left + ratio * away
                dirn[:, lanes] = fresh
                probe[:, lanes] = fresh.astype(jnp.bfloat16)

    outs = []
    for q in range(CHUNKS):
        for c in range(q * tiles // CHUNKS, (q + 1) * tiles // CHUNKS):
            lanes = slice(c * TILE, (c + 1) * TILE)
            srows[lanes, :] = (rs[:, lanes] + step * dirn[:, lanes]).T
            rst[lanes, :] = (left_field[:, lanes] - step * image[:, lanes]).T
        run = pl.ds(q * part, part)
        for n, (source, target) in enumerate(((srows, sol_hbm), (rst, res_hbm))):
            copy = pltpu.make_async_copy(source.at[run], target.at[run], out_sem.at[n, q])
            copy.start()
            outs.append(copy)
    for copy in outs:
        copy.wait()


def conjugate(right_side, point_order, leaf_blocks, bases, rank_weights, n_dev):
    columns, points = right_side.shape
    blocks, leaf_size, _ = leaf_blocks.shape
    levels, rank = rank_weights.shape
    upper = n_dev.bit_length() - 1
    local = levels - upper
    quarter = columns // 4
    starts = list(range(2, upper, 2))
    n_stage = len(starts)
    f32, bf16 = jnp.float32, jnp.bfloat16
    scratch = [
        pltpu.VMEM((columns, points), f32),
        pltpu.VMEM((points, columns), f32),
        pltpu.VMEM((TILE, columns), f32),
        pltpu.VMEM((points, columns), f32),
        pltpu.VMEM((blocks, leaf_size, leaf_size), bf16),
        pltpu.VMEM((levels * rank, points), bf16),
        pltpu.VMEM((columns, points), f32),
        pltpu.VMEM((columns, points), f32),
        pltpu.VMEM((columns, points), bf16),
        pltpu.VMEM((columns, points), f32),
        pltpu.VMEM((blocks, columns, local * rank), f32),
        pltpu.VMEM((blocks, columns, local * rank), bf16),
        pltpu.VMEM((columns, upper * rank), bf16),
        pltpu.VMEM((ITERS, upper, columns, rank), f32),
        pltpu.VMEM((ITERS, columns, rank), f32),
        pltpu.VMEM((ITERS, 3, upper - 1, quarter, rank), f32),
        pltpu.VMEM((ITERS, upper, columns, rank), f32),
        pltpu.VMEM((ITERS, n_stage + 1, 8, columns), f32),
        pltpu.VMEM((ITERS, 3 * (n_stage + 1), 8, columns), f32),
    ]
    scratch += [pltpu.VMEM((ITERS, upper - b, quarter, rank), f32) for b in starts]
    scratch += [pltpu.VMEM((ITERS, upper - b, quarter, rank), f32) for b in starts]
    scratch += [pltpu.VMEM((ITERS, 2, max(upper - b - 1, 1), quarter, rank), f32) for b in starts]
    slots = 7 + 6 * n_stage
    scratch += [
        pltpu.SemaphoreType.DMA((CHUNKS,)),
        pltpu.SemaphoreType.DMA,
        pltpu.SemaphoreType.DMA,
        pltpu.SemaphoreType.DMA((ITERS, slots)),
        pltpu.SemaphoreType.DMA((ITERS, slots)),
        pltpu.SemaphoreType.DMA((ITERS, 3 * (n_stage + 1))),
        pltpu.SemaphoreType.DMA((ITERS, 3 * (n_stage + 1))),
        pltpu.SemaphoreType.DMA((2, CHUNKS)),
    ]
    hbm = pl.BlockSpec(memory_space=pl.ANY)
    vmem = pl.BlockSpec(memory_space=pltpu.VMEM)
    shape = jax.ShapeDtypeStruct((points, columns), f32)
    return pl.pallas_call(
        functools.partial(cg_kernel, n_dev, levels, n_stage),
        out_shape=(shape, shape),
        in_specs=[hbm, pl.BlockSpec(memory_space=pltpu.SMEM), hbm, hbm, vmem],
        out_specs=(hbm, hbm),
        scratch_shapes=scratch,
        compiler_params=pltpu.CompilerParams(
            collective_id=0, has_side_effects=True, vmem_limit_bytes=56 * 2 ** 20
        ),
        name="cg",
    )(right_side, point_order, leaf_blocks, bases.reshape(levels * rank, points), rank_weights)


def scatter_kernel(order_ref, sol_hbm, res_hbm, out_sol, out_res, sol_in, res_in, sol_rows, res_rows,
                   sol_turn, res_turn, in_sem, out_sem):
    points, columns = sol_in.shape
    tiles = points // TILE
    part = points // CHUNKS
    copies = []
    for q in range(CHUNKS):
        run = pl.ds(q * part, part)
        pair = []
        for n, (source, target) in enumerate(((sol_hbm, sol_in), (res_hbm, res_in))):
            copy = pltpu.make_async_copy(source.at[run], target.at[run], in_sem.at[n, q])
            copy.start()
            pair.append(copy)
        copies.append(pair)

    def place(c, carry):
        at = pl.multiple_of(c * TILE, TILE)
        for j in range(TILE):
            target = order_ref[at + j] & (points - 1)
            sol_rows[pl.ds(target, 1), :] = sol_in[pl.ds(at + j, 1), :]
            res_rows[pl.ds(target, 1), :] = res_in[pl.ds(at + j, 1), :]
        return carry

    for q in range(CHUNKS):
        for copy in copies[q]:
            copy.wait()
        lax.fori_loop(q * tiles // CHUNKS, (q + 1) * tiles // CHUNKS, place, 0)

    outs = []
    for q in range(CHUNKS):
        for c in range(q * tiles // CHUNKS, (q + 1) * tiles // CHUNKS):
            lanes = slice(c * TILE, (c + 1) * TILE)
            sol_turn[:, lanes] = sol_rows[lanes, :].T
            res_turn[:, lanes] = res_rows[lanes, :].T
        run = pl.ds(q * part, part)
        for n, (source, target) in enumerate(((sol_turn, out_sol), (res_turn, out_res))):
            copy = pltpu.make_async_copy(source.at[:, run], target.at[:, run], out_sem.at[n, q])
            copy.start()
            outs.append(copy)
    for copy in outs:
        copy.wait()


def scatter_back(point_order, field, residual):
    points, columns = field.shape
    hbm = pl.BlockSpec(memory_space=pl.ANY)
    shape = jax.ShapeDtypeStruct((columns, points), jnp.float32)
    return pl.pallas_call(
        scatter_kernel,
        out_shape=(shape, shape),
        in_specs=[pl.BlockSpec(memory_space=pltpu.SMEM), hbm, hbm],
        out_specs=(hbm, hbm),
        scratch_shapes=[pltpu.VMEM((points, columns), jnp.float32)] * 4
        + [pltpu.VMEM((columns, points), jnp.float32)] * 2
        + [pltpu.SemaphoreType.DMA((2, CHUNKS))] * 2,
        compiler_params=pltpu.CompilerParams(vmem_limit_bytes=56 * 2 ** 20),
        name="place",
    )(point_order, field, residual)


def on_device(right_side, point_order, leaf_blocks, bases, rank_weights, n_dev):
    field, residual = conjugate(right_side, point_order, leaf_blocks, bases, rank_weights, n_dev)
    return scatter_back(point_order, field, residual)


def solution(mesh):
    return jax.shard_map(
        functools.partial(on_device, n_dev=mesh.shape["leaf"]),
        mesh=mesh,
        in_specs=(
            P("groups", "leaf"),
            P(("groups", "leaf")),
            P("leaf", None, None),
            P(None, None, "leaf"),
            P(),
        ),
        out_specs=(P("groups", "leaf"), P("groups", "leaf")),
        check_vma=False,
    )
```

time: 76.5 us -> 63.1 us (0.82)
  Pallas kernels: 72.4 us -> 62.2 us
  local copies, waits for them, and re-layouts: 3.18 us -> 0 us
    pallas_call x1, Pallas kernels: 58.6 us -> 52 us  [conjugate(): pl.pallas_call(functools.partial(cg_kernel, n_dev, levels, n_stage), out_...]
    pallas_call x1, Pallas kernels: 13.8 us -> 10.1 us  [scatter_back(): pl.pallas_call(scatter_kernel, out_shape=(shape, shape), in_specs=[pl.Blo...]
    unnamed x6 -> x0, local copies, waits for them, and re-layouts: 3.18 us -> none
where the time goes in v2:
time: 63.1 us; the launch traced here: 62.8 us
  Pallas kernels  62.2 us (99%)
  between operations  0.64 us (1%)
    pallas_call x1, Pallas kernels, conjugate(): pl.pallas_call(functools.partial(cg_kernel, n_dev, levels, n_stage), out_...  52 us
    pallas_call x1, Pallas kernels, scatter_back(): pl.pallas_call(scatter_kernel, out_shape=(shape, shape), in_specs=[pl.Blo...  10.1 us

profile of v2, /device:TPU:0, one launch (start us, length us, event | category | flops | bytes accessed | tf_op | source)
XLA Modules:
  0.0 62.8 jit_solution(5581317465450890217)
XLA Ops:
  0.6 52.0 %cg.1 = (f32[4096,128]{1,0:T(8,128)}, f32[4096,128]{1,0:T(8,128)}) custom-call(f32[128,4096]{1,0:T(8,128)} %refs_0_.1, s32[4096]{0:T(1024)} %order_ref.1, bf16[8,512,512]{2,1,0:T(8,128)(2,1)} %refs_2_.1, bf16[896,4096]{1,0:T(8,128)(2,1)} %bitcast.1, f32[7,128]{1,0:T(8,128)} %refs_4_.1), custom_call_target="tpu_custom_call" | custom-call | tf_op jit(solution)/shard_map/cg/pallas_call | solution.py:360
  52.6 10.1 %place.1 = (f32[128,4096]{1,0:T(8,128)}, f32[128,4096]{1,0:T(8,128)}) custom-call(s32[4096]{0:T(1024)} %order_ref.1, f32[4096,128]{1,0:T(8,128)} %get-tuple-element.4.sol_hbm, f32[4096,128]{1,0:T(8,128)} %get-tuple-element.5.res_hbm), custom_call_target="tpu_custom_call" | custom-call | tf_op jit(solution)/shard_map/place/pallas_call | solution.py:420

commit v3 on v2

--- a/solution.py
+++ b/solution.py
@@ -42,7 +42,7 @@
 
     rs_hbm, order_ref, leaf_hbm, bases_hbm, weights_ref, sol_hbm, res_hbm = grab(7)
     rs, rst, rows, srows, leaf, bases, dirn, left_field, probe, image, coef, low_s, up_s = grab(13)
-    pend0, recv_a, recv_q, total, vec_out, vec_in = grab(6)
+    pend0, recv_a, recv_q, total, products, vec_out, vec_in = grab(7)
     pends, firsts, others = grab(n_stage), grab(n_stage), grab(n_stage)
     rs_sem, leaf_sem, bases_sem, send_sem, recv_sem, vsend_sem, vrecv_sem, out_sem = grab(8)
 
@@ -216,64 +216,83 @@
                     low_s[b, :, lanes] = value
         if it == 0:
             leaf_copy.wait()
+        curve = jnp.zeros((columns, TILE), jnp.float32)
+        norm = jnp.zeros((columns, TILE), jnp.float32)
+        power = jnp.zeros((columns, TILE), jnp.float32)
+        last = it + 1 == ITERS
         for b in range(blocks):
             span = slice(b * leaf_size, (b + 1) * leaf_size)
-            image[:, span] = nn_dot(probe[:, span], leaf[b]) + nn_dot(low_s[b], bases[:low, span])
+            field = nn_dot(probe[:, span], leaf[b]) + nn_dot(low_s[b], bases[:low, span])
+            image[:, span] = field
+            if last:
+                for c in range(leaf_size // TILE):
+                    at = b * leaf_size + c * TILE
+                    curve = curve + dirn[:, at:at + TILE] * field[:, c * TILE:(c + 1) * TILE]
+                    left = left_field[:, at:at + TILE]
+                    norm = norm + left * left
             if b == blocks - 3:
                 advance()
         for _ in range(n_stage):
             advance()
+
+        def vector(k):
+            return pltpu.make_async_remote_copy(
+                src_ref=vec_out.at[it],
+                dst_ref=vec_in.at[it, k],
+                send_sem=vsend_sem.at[it, k],
+                recv_sem=vrecv_sem.at[it, k],
+                device_id={"leaf": (me + k) % n_dev},
+                device_id_type=MESH,
+            )
+
+        def push(k, carry):
+            vector(k).start()
+            return carry
+
+        def take(k, carry):
+            vector(k).wait()
+            return carry + vec_in[it, k]
+
+        def publish():
+            vec_out[it, 0:1, :] = row_of(curve)
+            vec_out[it, 1:2, :] = row_of(norm)
+            vec_out[it, 2:3, :] = row_of(power)
+            vec_out[it, 3:8, :] = jnp.zeros((5, TILE), jnp.float32)
+            lax.fori_loop(1, n_dev, push, 0)
+
+        if last:
+            shared = total[it, 0]
+            products[...] = curve + 0.5 * shared * scaled(shared, local).astype(jnp.float32)
+            own = jnp.zeros((quarter, rank), jnp.float32)
+            for u in range(1, upper):
+                held = total[it, u, mine]
+                own = own + 0.5 ** (u - 1) * held * scaled(held, local + u).astype(jnp.float32)
+            products[mine] = products[mine] + own
+            curve = products[...]
+            publish()
         for copy in state["back"]:
             copy.wait_recv()
         for u in range(upper):
             up_s[:, u * rank:(u + 1) * rank] = scaled(total[it, u], local + u)
 
-        curve = jnp.zeros((columns, TILE), jnp.float32)
-        norm = jnp.zeros((columns, TILE), jnp.float32)
-        power = jnp.zeros((columns, TILE), jnp.float32)
-        held = dirn if it == 0 else left_field
         for b in range(blocks):
             span = slice(b * leaf_size, (b + 1) * leaf_size)
             field = image[:, span] + nn_dot(up_s[...], bases[low:, span])
             image[:, span] = field
-            for c in range(leaf_size // TILE):
-                at = b * leaf_size + c * TILE
-                piece = field[:, c * TILE:(c + 1) * TILE]
-                away = dirn[:, at:at + TILE]
-                curve = curve + away * piece
-                left = held[:, at:at + TILE]
-                norm = norm + left * left
-                if it + 1 < ITERS:
+            if not last:
+                for c in range(leaf_size // TILE):
+                    at = b * leaf_size + c * TILE
+                    piece = field[:, c * TILE:(c + 1) * TILE]
+                    away = dirn[:, at:at + TILE]
+                    left = away if it == 0 else left_field[:, at:at + TILE]
+                    curve = curve + away * piece
+                    norm = norm + left * left
                     power = power + piece * piece
-        vec_out[it, 0, 0:1, :] = row_of(curve)
-        vec_out[it, 0, 1:2, :] = row_of(norm)
-        vec_out[it, 0, 2:3, :] = row_of(power)
-        vec_out[it, 0, 3:8, :] = jnp.zeros((5, TILE), jnp.float32)
-        for stage in range(n_stage + 1):
-            bit = 2 * stage
-            peers = (3, 2, 1) if bit + 1 < upper else (1,)
-            hops = []
-            for k in peers:
-                slot = stage * 3 + k - 1
-                hop = pltpu.make_async_remote_copy(
-                    src_ref=vec_out.at[it, stage],
-                    dst_ref=vec_in.at[it, slot],
-                    send_sem=vsend_sem.at[it, slot],
-                    recv_sem=vrecv_sem.at[it, slot],
-                    device_id={"leaf": flip(k, bit)},
-                    device_id_type=MESH,
-                )
-                hop.start()
-                hops.append(hop)
-            if stage == 0:
-                for copy in sent:
-                    copy.wait_send()
-            sums = vec_out[it, stage]
-            for hop, k in zip(hops, peers):
-                hop.wait()
-                sums = sums + vec_in[it, stage * 3 + k - 1]
-            if stage < n_stage:
-                vec_out[it, stage + 1] = sums
+        if not last:
+            publish()
+        for copy in sent:
+            copy.wait_send()
+        sums = lax.fori_loop(1, n_dev, take, vec_out[it])
         curvature, norm_now, squares = sums[0:1], sums[1:2], sums[2:3]
         step_row = norm_now / curvature
         step = spread(step_row)
@@ -337,8 +356,9 @@
         pltpu.VMEM((ITERS, columns, rank), f32),
         pltpu.VMEM((ITERS, 3, upper - 1, quarter, rank), f32),
         pltpu.VMEM((ITERS, upper, columns, rank), f32),
-        pltpu.VMEM((ITERS, n_stage + 1, 8, columns), f32),
-        pltpu.VMEM((ITERS, 3 * (n_stage + 1), 8, columns), f32),
+        pltpu.VMEM((columns, rank), f32),
+        pltpu.VMEM((ITERS, 8, columns), f32),
+        pltpu.VMEM((ITERS, n_dev, 8, columns), f32),
     ]
     scratch += [pltpu.VMEM((ITERS, upper - b, quarter, rank), f32) for b in starts]
     scratch += [pltpu.VMEM((ITERS, upper - b, quarter, rank), f32) for b in starts]
@@ -350,8 +370,8 @@
         pltpu.SemaphoreType.DMA,
         pltpu.SemaphoreType.DMA((ITERS, slots)),
         pltpu.SemaphoreType.DMA((ITERS, slots)),
-        pltpu.SemaphoreType.DMA((ITERS, 3 * (n_stage + 1))),
-        pltpu.SemaphoreType.DMA((ITERS, 3 * (n_stage + 1))),
+        pltpu.SemaphoreType.DMA((ITERS, n_dev)),
+        pltpu.SemaphoreType.DMA((ITERS, n_dev)),
         pltpu.SemaphoreType.DMA((2, CHUNKS)),
     ]
     hbm = pl.BlockSpec(memory_space=pl.ANY)

time: 63.1 us -> 58.2 us (0.922)
  Pallas kernels: 62.2 us -> 57.2 us
    pallas_call x1, Pallas kernels: 52 us -> 47.1 us  [conjugate(): pl.pallas_call(functools.partial(cg_kernel, n_dev, levels, n_stage), out_...]
where the time goes in v3:
time: 58.2 us; the launch traced here: 57.9 us
  Pallas kernels  57.2 us (98%)
  between operations  0.64 us (1%)
    pallas_call x1, Pallas kernels, conjugate(): pl.pallas_call(functools.partial(cg_kernel, n_dev, levels, n_stage), out_...  47.1 us
    pallas_call x1, Pallas kernels, scatter_back(): pl.pallas_call(scatter_kernel, out_shape=(shape, shape), in_specs=[pl.Blo...  10.1 us

profile of v3, /device:TPU:0, one launch (start us, length us, event | category | flops | bytes accessed | tf_op | source)
XLA Modules:
  0.0 57.9 jit_solution(7353262373404950359)
XLA Ops:
  0.6 47.1 %cg.1 = (f32[4096,128]{1,0:T(8,128)}, f32[4096,128]{1,0:T(8,128)}) custom-call(f32[128,4096]{1,0:T(8,128)} %refs_0_.1, s32[4096]{0:T(1024)} %order_ref.1, bf16[8,512,512]{2,1,0:T(8,128)(2,1)} %refs_2_.1, bf16[896,4096]{1,0:T(8,128)(2,1)} %bitcast.1, f32[7,128]{1,0:T(8,128)} %refs_4_.1), custom_call_target="tpu_custom_call" | custom-call | tf_op jit(solution)/shard_map/cg/pallas_call | solution.py:380
  47.7 10.1 %place.1 = (f32[128,4096]{1,0:T(8,128)}, f32[128,4096]{1,0:T(8,128)}) custom-call(s32[4096]{0:T(1024)} %order_ref.1, f32[4096,128]{1,0:T(8,128)} %get-tuple-element.4.sol_hbm, f32[4096,128]{1,0:T(8,128)} %get-tuple-element.5.res_hbm), custom_call_target="tpu_custom_call" | custom-call | tf_op jit(solution)/shard_map/place/pallas_call | solution.py:440

commit v4 on v3

--- a/solution.py
+++ b/solution.py
@@ -10,7 +10,7 @@
 
 ITERS = 2
 TILE = 128
-CHUNKS = 4
+CHUNKS = 8
 MESH = pl.DeviceIdType.MESH
 
 

time: 58.2 us -> 58.2 us (level)
  no operation moved by 1% of the time
where the time goes in v4:
time: 58.2 us; the launch traced here: 57.8 us
  Pallas kernels  57.2 us (98%)
  between operations  0.64 us (1%)
    pallas_call x1, Pallas kernels, conjugate(): pl.pallas_call(functools.partial(cg_kernel, n_dev, levels, n_stage), out_...  47.2 us
    pallas_call x1, Pallas kernels, scatter_back(): pl.pallas_call(scatter_kernel, out_shape=(shape, shape), in_specs=[pl.Blo...  9.98 us

profile of v4, /device:TPU:0, one launch (start us, length us, event | category | flops | bytes accessed | tf_op | source)
XLA Modules:
  0.0 57.8 jit_solution(12033706797650304015)
XLA Ops:
  0.6 47.2 %cg.1 = (f32[4096,128]{1,0:T(8,128)}, f32[4096,128]{1,0:T(8,128)}) custom-call(f32[128,4096]{1,0:T(8,128)} %refs_0_.1, s32[4096]{0:T(1024)} %order_ref.1, bf16[8,512,512]{2,1,0:T(8,128)(2,1)} %refs_2_.1, bf16[896,4096]{1,0:T(8,128)(2,1)} %bitcast.1, f32[7,128]{1,0:T(8,128)} %refs_4_.1), custom_call_target="tpu_custom_call" | custom-call | tf_op jit(solution)/shard_map/cg/pallas_call | solution.py:380
  47.9 10.0 %place.1 = (f32[128,4096]{1,0:T(8,128)}, f32[128,4096]{1,0:T(8,128)}) custom-call(s32[4096]{0:T(1024)} %order_ref.1, f32[4096,128]{1,0:T(8,128)} %get-tuple-element.4.sol_hbm, f32[4096,128]{1,0:T(8,128)} %get-tuple-element.5.res_hbm), custom_call_target="tpu_custom_call" | custom-call | tf_op jit(solution)/shard_map/place/pallas_call | solution.py:440
